TPU v7x, 256 devices: a whole 4x4x8 slice. The times are simulated.
256 devices in a mesh: row: 64 (over z, y, core), col: 4 (over x).
Axes of the slice: x: 4, y: 4, z: 8, core: 2. Of those that a mesh axis runs over, the one named last changes fastest.
Arguments:
- panel_block: float32 [131072, 128], P(('row', 'col')), may hold values from -360 to 360
- trailing: float32 [131072, 2048], P('row', 'col'), may hold values from -2048 to 2048
Outputs:
- r_scaled: float32 [128, 128], replicated
- w_scaled: float32 [128, 2048], P(None, 'col')
- remainder: float32 [131072, 2048], P('row', 'col')
All inputs are finite; a program needn't handle non-finite values.
Results may differ from a plain program's by a relative error of at most 0.0003.
Values sent between devices are 32-bit elements; how exact they have to be, the bound alone decides.
A program may use at most 64 MiB of HBM per device.

v0:
```python
import math

import jax
import jax.numpy as jnp
from jax import lax
from jax.sharding import PartitionSpec as P


def inner_rows(first_block, second_block):
    return jnp.einsum("rk,rc->kc", first_block, second_block, precision=lax.Precision.HIGHEST)


def upper_factor(gram):
    width = gram.shape[0]
    positions = lax.iota(jnp.int32, width)

    def column_step(index, state):
        remaining, lower = state
        picker = (positions == index).astype(jnp.float32)
        column = jnp.dot(remaining, picker, precision=lax.Precision.HIGHEST)
        pivot = jnp.sum(column * picker)
        column = jnp.where(positions >= index, column / jnp.sqrt(pivot), 0.0)
        remaining = remaining - column[:, None] * column[None, :]
        lower = lower + column[:, None] * picker[None, :]
        return (remaining, lower)

    start = (gram, jnp.zeros_like(gram))
    remaining, lower = lax.fori_loop(0, width, column_step, start)
    return lower.T


def upper_inverse(factor):
    width = factor.shape[0]
    positions = lax.iota(jnp.int32, width)

    def row_step(count, inverse):
        index = width - 1 - count
        picker = (positions == index).astype(jnp.float32)
        factor_row = jnp.dot(picker, factor, precision=lax.Precision.HIGHEST)
        pivot = jnp.sum(factor_row * picker)
        new_row = (picker - jnp.dot(factor_row, inverse, precision=lax.Precision.HIGHEST)) / pivot
        return inverse + picker[:, None] * new_row[None, :]

    return lax.fori_loop(0, width, row_step, jnp.zeros_like(factor))


def body(panel_block, trailing):
    total_rows = panel_block.shape[0] * lax.axis_size("row") * lax.axis_size("col")
    norm_scale = 1.0 / math.sqrt(total_rows)
    gathered = lax.all_gather(panel_block, "col", axis=0, tiled=True)
    local_gram = inner_rows(panel_block, panel_block)
    gram = lax.psum(local_gram, ("row", "col"))
    factor = upper_factor(gram)
    inverse = upper_inverse(factor)
    basis = jnp.dot(gathered, inverse, precision=lax.Precision.HIGHEST)
    weights = lax.psum(inner_rows(basis, trailing), "row")
    remainder = trailing - jnp.dot(basis, weights, precision=lax.Precision.HIGHEST)
    return (factor * norm_scale, weights * norm_scale, remainder)


def solution(mesh):
    in_specs = (P(("row", "col"), None), P("row", "col"))
    out_specs = (P(), P(None, "col"), P("row", "col"))
    return jax.shard_map(body, mesh=mesh, in_specs=in_specs, out_specs=out_specs, check_vma=False)
```

profile of v0, /device:TPU:1, one launch (start us, length us, event | category | flops | bytes accessed | tf_op | source)
XLA Modules:
  0.0 1168.4 jit_solution(3138111512083544413)
XLA Ops:
  8.0 2.3 fusion.21
  11.0 247.1 %all-reduce.3.cloned.1.call-done = f32[128,128]{1,0:T(8,128)} async-done(((f32[128,128]{1,0:T(8,128)}), f32[128,128]{1,0:T(8,128)}) %all-reduce.3.cloned.1.call-update) | async-done | bytes 65552 | tf_op jit(solution)/shard_map/psum | solution.py:52
  258.1 499.7 %while.32 = (s32[]{:T(128)}, f32[128,128]{1,0:T(8,128)}, f32[128,128]{1,0:T(8,128)S(1)}, s32[]{:T(128)}, s32[]{:T(128)}) while((s32[]{:T(128)}, f32[128,128]{1,0:T(8,128)}, f32[128,128]{1,0:T(8,128)S(1)}, s32[]{:T(128)}, s32[]{:T(128)}) %tuple.75), condition=%wide.region_3.4_spmd.clone.clone, body=%wide.region_1.3_spmd.clone.clone.sunk | while | flops 279682 | bytes 330851 | solution.py:28
  258.1 1.6 fusion.51
  262.0 1.6 fusion.51
  265.9 1.6 fusion.51
  269.8 1.6 fusion.51
  273.7 1.6 fusion.51
  277.6 1.6 fusion.51
  281.5 1.6 fusion.51
  285.4 1.6 fusion.51
  289.3 1.6 fusion.51
  293.2 1.6 fusion.51
  297.1 1.6 fusion.51
  301.0 1.6 fusion.51
  304.9 1.6 fusion.51
  308.8 1.6 fusion.51
  312.7 1.6 fusion.51
  320.5 1.6 fusion.51
  324.4 1.6 fusion.51
  328.3 1.6 fusion.51
  332.2 1.6 fusion.51
  336.1 1.6 fusion.51
  340.0 1.6 fusion.51
  344.0 1.6 fusion.51
  347.9 1.6 fusion.51
  351.8 1.6 fusion.51
  355.7 1.6 fusion.51
  359.6 1.6 fusion.51
  363.5 1.6 fusion.51
  367.4 1.6 fusion.51
  371.3 1.6 fusion.51
  375.2 1.6 fusion.51
  379.1 1.6 fusion.51
  383.0 1.6 fusion.51
  386.9 1.6 fusion.51
  394.7 1.6 fusion.51
  398.6 1.6 fusion.51
  402.5 1.6 fusion.51
  406.4 1.6 fusion.51
  410.3 1.6 fusion.51
  414.2 1.6 fusion.51
  418.1 1.6 fusion.51
  422.0 1.6 fusion.51
  425.9 1.6 fusion.51
  429.8 1.6 fusion.51
  433.7 1.6 fusion.51
  437.6 1.6 fusion.51
  441.5 1.6 fusion.51
  445.4 1.6 fusion.51
  449.4 1.6 fusion.51
  453.3 1.6 fusion.51
  457.2 1.6 fusion.51
  461.1 1.6 fusion.51
  468.9 1.6 fusion.51
  472.8 1.6 fusion.51
  476.7 1.6 fusion.51
  480.6 1.6 fusion.51
  484.5 1.6 fusion.51
  757.8 216.0 %while.31 = (s32[]{:T(128)}, f32[128,128]{1,0:T(8,128)S(1)}, f32[128,128]{1,0:T(8,128)S(1)}, s32[]{:T(128)}, s32[]{:T(128)}, /*index=5*/s32[]{:T(128)}) while((s32[]{:T(128)}, f32[128,128]{1,0:T(8,128)S(1)}, f32[128,128]{1,0:T(8,128)S(1)}, s32[]{:T(128)}, s32[]{:T(128)}, /*index=5*/s32[]{:T(128)}) %tuple.87), condition=%wide.region_6.7_spmd.clone, body=%wide.region_4.6_spmd.clone.sunk | while | flops 460035 | bytes 265328 | solution.py:44
  973.9 2.3 fusion.22
  976.2 5.3 fusion.23
  982.2 171.0 %all-reduce.5.cloned.1.call-done = f32[128,512]{1,0:T(8,128)} async-done(((f32[128,512]{1,0:T(8,128)}), f32[128,512]{1,0:T(8,128)}) %all-reduce.5.cloned.1.call-update) | async-done | bytes 262160 | tf_op jit(solution)/shard_map/psum | solution.py:56
  1153.2 7.0 convolution_subtract_fusion
  (982 shorter events, 531.1 us)
Async XLA Ops:
  8.0 250.1 %all-reduce.3.cloned.1.call-start = ((), (), s32[]{:S(2)}) async-start(), calls=%async_computation | async-start | bytes 131072 | tf_op jit(solution)/shard_map/psum | solution.py:52
  10.3 963.6 %all-gather.2.cloned.1.call-start = ((), (), s32[]{:S(2)}) async-start(), calls=%async_computation.1 | async-start | bytes 1310720 | tf_op jit(solution)/shard_map/all_gather | solution.py:50
  10.9 1142.3 %all-reduce.5.cloned.1.call-start = ((), (), s32[]{:S(2)}) async-start(), calls=%async_computation.2 | async-start | bytes 524288 | tf_op jit(solution)/shard_map/psum | solution.py:56
  1153.2 7.0 copy-start
Sparse Core Ops, SparseCore 0:
  14.9 243.1 all-reduce.2
  981.7 171.4 all-reduce.4
Sparse Core Ops, SparseCore 1:
  12.6 28.4 all-gather.1
where the time goes:
time: 1180 us; the launch traced here: 1170 us
  matrix products  424 us (36%)
  waiting for transfers between devices  419 us (36%)
  other arithmetic  214 us (18%)
  loops' own time  95.4 us (8%)
  between operations  15.5 us (1%)
    psum x1, waiting for transfers between devices, body(): gram = lax.psum(local_gram, ('row', 'col'))  247 us
    dot_general x128, matrix products, column_step(): column = jnp.dot(remaining, picker, precision=lax.Precision.HIGHEST)  209 us
    add x128, other arithmetic, column_step(): lower = lower + column[:, None] * picker[None, :]  198 us
    psum x1, waiting for transfers between devices, body(): weights = lax.psum(inner_rows(basis, trailing), 'row')  171 us
    dot_general x128, matrix products, row_step(): jnp.dot(factor_row, inverse, precision=lax.Precision.HIGHEST)  102 us
    dot_general x128, matrix products, row_step(): factor_row = jnp.dot(picker, factor, precision=lax.Precision.HIGHEST)  96.5 us
    another operation x1, loops' own time, upper_factor(): remaining, lower = lax.fori_loop(0, width, column_step, start)  91.4 us
  transfers between devices with their start and end apart: 3, of which 2 were waited for; matrix products, arithmetic and copies ran while one was open for 53% of the time, Pallas kernels for 0%

commit v1 on v0

v1 whole, which is shorter than its diff:
```python
import math

import jax
import jax.numpy as jnp
from jax import lax
from jax.experimental import pallas as pl
from jax.experimental.pallas import tpu as pltpu
from jax.sharding import PartitionSpec as P

F32 = jnp.float32
BF16 = jnp.bfloat16
MESH = pl.DeviceIdType.MESH
HIGHEST = lax.Precision.HIGHEST
NB = 128
Y_DIM, Z_DIM, X_DIM = 4, 8, 4
CHIPS = Y_DIM * Z_DIM
ROWS_OWN = 512
COLS_OWN = 512
HALF = ROWS_OWN // 2


def reciprocal(p):
    r = pl.reciprocal(p, approx=True)
    return r * (2.0 - p * r)


def lane_spread(v, c):
    return jnp.broadcast_to(v[:, c : c + 1], (8, NB))


def row_spread(v, j):
    return jnp.broadcast_to(v[j : j + 1, :], (8, NB))


def factor_steps(g, r_ref, y_ref):
    sub = lax.broadcasted_iota(jnp.int32, (8, NB), 0)
    lane = lax.broadcasted_iota(jnp.int32, (8, NB), 1)
    n = NB // 8
    left = [g[i] for i in range(n)]
    right = [jnp.where(lane == sub + 8 * i, 1.0, 0.0) for i in range(n)]
    for k in range(n):
        v, w = left[k], right[k]
        diag = [lane_spread(v, 8 * k + j) for j in range(8)]
        more = k + 1 < n
        if more:
            diag2 = [lane_spread(left[k + 1], 8 * k + j) for j in range(8)]
            v2, w2 = left[k + 1], right[k + 1]
        pivots = jnp.ones((8, NB), F32)
        for j in range(8):
            p = row_spread(diag[j], j)
            r = reciprocal(p)
            m = jnp.where(sub > j, diag[j] * r, 0.0)
            vj, wj = row_spread(v, j), row_spread(w, j)
            v = v - m * vj
            w = w - m * wj
            if more:
                m2 = diag2[j] * r
                v2 = v2 - m2 * vj
                w2 = w2 - m2 * wj
            for jj in range(j + 1, 8):
                c = row_spread(diag[jj], j)
                diag[jj] = diag[jj] - m * c
                if more:
                    diag2[jj] = diag2[jj] - m2 * c
            pivots = jnp.where(sub == j, p, pivots)
        scale = lax.rsqrt(pivots)
        u = jnp.where(lane >= 8 * k + sub, v * scale, 0.0)
        z = w * scale
        r_ref[8 * k : 8 * k + 8, :] = u
        y_ref[8 * k : 8 * k + 8, :] = z
        if more:
            left[k + 1], right[k + 1] = v2, w2
        if k + 2 < n:
            ut = u.T
            us = [row_spread(u, j) for j in range(8)]
            zs = [row_spread(z, j) for j in range(8)]
            for i in range(k + 2, n):
                t = ut[8 * i : 8 * i + 8, :]
                a, b = left[i], right[i]
                for j in range(8):
                    tj = jnp.broadcast_to(t[:, j : j + 1], (8, NB))
                    a = a - tj * us[j]
                    b = b - tj * zs[j]
                left[i], right[i] = a, b
        yield


def split(x):
    hi = x.astype(BF16)
    return hi, (x - hi.astype(F32)).astype(BF16)


def inner(a, b, precision=None):
    return lax.dot_general(a, b, (((0,), (0,)), ((), ())), precision=precision, preferred_element_type=F32)


def main_kernel(
    p_hbm, t_hbm,
    r_ref, w_ref, xh_ref, xl_ref, phl_ref, t_ref,
    pg, thl, gbuf, abuf, bbuf, tile, gfull, y_ref, sbuf, cbuf, sred, rbuf, sfull,
    load_sem, gsend, grecv, esend, erecv,
):
    row = lax.axis_index("row")
    col = lax.axis_index("col")
    core = lax.rem(row, 2)
    chip = lax.div(row, 2)
    y = lax.rem(chip, Y_DIM)
    z = lax.div(chip, Y_DIM)
    right, left, across = (lax.rem(col + d, X_DIM) for d in (1, 3, 2))

    def device(z_, y_, core_):
        return (z_ * Y_DIM + y_) * 2 + core_

    sibling = (row + 1 - 2 * core, col)

    def zc_peer(d):
        q = lax.rem(z * 2 + core + d, 2 * Z_DIM)
        return q, (device(lax.div(q, 2), y, lax.rem(q, 2)), col)

    def yx_peer(d):
        s = lax.rem(y * X_DIM + col + d, Y_DIM * X_DIM)
        return s, (device(z, lax.div(s, X_DIM), core), lax.rem(s, X_DIM))

    def chip_peer(d):
        m = lax.rem(chip + d, CHIPS)
        return m, (m * 2 + core, col)

    me_q = z * 2 + core
    me_s = y * X_DIM + col

    def load_p():
        return pltpu.make_async_copy(p_hbm, pg.at[col], load_sem.at[4])

    def load_t(b, k):
        rows = pl.ds(pl.multiple_of(b * ROWS_OWN, ROWS_OWN), ROWS_OWN)
        return pltpu.make_async_copy(t_hbm.at[rows, :], t_ref.at[rows, :], load_sem.at[k])

    load_p().start()
    order = (col, left, right, across)
    for k, b in enumerate(order):
        load_t(b, k).start()

    barrier = pltpu.get_barrier_semaphore()

    def greet(peer):
        pl.semaphore_signal(barrier, inc=1, device_id=peer, device_id_type=MESH)

    def each(lo, hi, f):
        def step(d, c):
            f(d)
            return c

        lax.fori_loop(lo, hi, step, 0)

    each(1, CHIPS, lambda d: greet(chip_peer(d)[1]))
    each(0, Z_DIM, lambda d: greet((device(d, y, 1 - core), col)))
    each(1, X_DIM, lambda dx: each(0, Y_DIM, lambda d: greet((device(z, d, core), lax.rem(col + dx, X_DIM)))))

    load_p().wait()
    own = pg[col]
    gram = inner(own, own, HIGHEST)
    gbuf[...] = gram.reshape(NB // 8, 8, NB)
    pl.semaphore_wait(barrier, CHIPS - 1 + Z_DIM + (X_DIM - 1) * Y_DIM)

    def remote(src, dst, send, recv, peer):
        return pltpu.make_async_remote_copy(
            src_ref=src, dst_ref=dst, send_sem=send, recv_sem=recv, device_id=peer, device_id_type=MESH
        )

    def send_a(d):
        q, peer = zc_peer(d)
        remote(gbuf.at[q], abuf.at[d - 1], esend.at[0], erecv.at[0], peer).start()

    each(1, 2 * Z_DIM, send_a)

    top, bottom = pl.ds(0, HALF), pl.ds(HALF, HALF)

    def ring(k, block, part, to):
        return remote(pg.at[block, part, :], pg.at[block, part, :], gsend.at[k], grecv.at[k], (row, to))

    ring(0, col, top, right).start()
    ring(1, col, bottom, left).start()
    ring(2, col, bottom, right).start()
    ring(3, col, top, left).start()

    def split_t(k, b):
        load_t(b, k).wait()
        rows = pl.ds(pl.multiple_of(b * ROWS_OWN, ROWS_OWN), ROWS_OWN)
        hi, lo = split(t_ref[rows, :])
        thl[0, rows, :] = hi
        thl[1, rows, :] = lo

    def product(b, first=False):
        rows = pl.ds(pl.multiple_of(b * ROWS_OWN, ROWS_OWN), ROWS_OWN)
        hi, lo = split(pg[b])
        phl_ref[rows, 0:NB] = hi
        phl_ref[rows, NB : 2 * NB] = lo
        th = thl[0, rows, :]
        s = inner(hi, th) + inner(lo, th) + inner(hi, thl[1, rows, :])
        for j in range(4):
            t = s[:, NB * j : NB * (j + 1)].reshape(16, 8, NB)
            at = slice(16 * j, 16 * (j + 1))
            sbuf[at] = t if first else sbuf[at] + t

    split_t(0, order[0])
    product(col, True)

    def received(k, buf):
        remote(buf, buf, esend.at[k], erecv.at[k], sibling).wait_recv()

    def sent(k, buf):
        remote(buf, buf, esend.at[k], erecv.at[k], sibling).wait_send()

    n_zc, n_yx = 2 * Z_DIM - 1, Y_DIM * X_DIM - 1
    received(0, abuf)
    bbuf[me_s] = gbuf[me_q] + jnp.sum(abuf[...], axis=0)

    def send_b(d):
        _, peer = yx_peer(d)
        remote(bbuf.at[me_s], bbuf.at[me_s], esend.at[1], erecv.at[1], peer).start()

    each(1, n_yx + 1, send_b)

    split_t(1, order[1])
    split_t(2, order[2])

    ring(0, left, top, right).wait_recv()
    ring(4, left, top, right).start()
    ring(1, right, bottom, left).wait_recv()
    ring(5, right, bottom, left).start()

    received(1, bbuf.at[pl.ds(0, n_yx)])
    gfull[me_q] = jnp.sum(bbuf[...], axis=0)

    def send_c(d):
        _, peer = zc_peer(d)
        remote(gfull.at[me_q], gfull.at[me_q], esend.at[2], erecv.at[2], peer).start()

    each(1, n_zc + 1, send_c)

    split_t(3, order[3])
    ring(2, left, bottom, right).wait_recv()
    product(left)
    ring(3, right, top, left).wait_recv()
    product(right)

    received(2, gfull.at[pl.ds(0, n_zc)])
    steps = factor_steps([gfull[i] for i in range(NB // 8)], r_ref, y_ref)

    def factor(count):
        for _ in range(count):
            next(steps)

    factor(3)
    ring(4, across, top, right).wait_recv()
    ring(5, across, bottom, left).wait_recv()
    product(across)

    mine = pl.ds(pl.multiple_of(core * CHIPS, CHIPS), CHIPS)
    other = pl.ds(pl.multiple_of((1 - core) * CHIPS, CHIPS), CHIPS)
    swap = remote(sbuf.at[other], cbuf, esend.at[3], erecv.at[3], sibling)
    swap.start()
    factor(3)
    swap.wait_recv()
    sred[...] = sbuf[mine] + cbuf[...]

    def send_rs(d):
        m, peer = chip_peer(d)
        remote(sred.at[m], rbuf.at[d - 1], esend.at[4], erecv.at[4], peer).start()

    each(1, CHIPS, send_rs)
    factor(6)
    received(4, rbuf)
    slot = core * CHIPS + chip
    sfull[slot] = sred[chip] + jnp.sum(rbuf[...], axis=0)

    def send_ag(d):
        _, peer = chip_peer(d)
        remote(sfull.at[slot], sfull.at[slot], esend.at[5], erecv.at[5], peer).start()

    each(1, CHIPS, send_ag)
    factor(4)
    received(5, sfull.at[pl.ds(0, CHIPS - 1)])
    last = remote(sfull.at[mine], sfull.at[mine], esend.at[6], erecv.at[6], sibling)
    last.start()

    for k, block, part, to in (
        (0, col, top, right), (1, col, bottom, left), (2, col, bottom, right),
        (3, col, top, left), (4, left, top, right), (5, right, bottom, left),
    ):
        ring(k, block, part, to).wait_send()
    sent(0, abuf)
    sent(1, bbuf.at[pl.ds(0, n_yx)])
    sent(2, gfull.at[pl.ds(0, n_zc)])
    swap.wait_send()
    sent(4, rbuf)
    sent(5, sfull.at[pl.ds(0, CHIPS - 1)])

    last.wait()
    s = jnp.concatenate([sfull[16 * j : 16 * (j + 1)].reshape(NB, NB) for j in range(4)], axis=1)
    inv_t = y_ref[...]
    w = jnp.dot(inv_t, s, precision=HIGHEST, preferred_element_type=F32)
    w_ref[...] = w
    hi, lo = split(inner(inv_t, w, HIGHEST))
    xh_ref[...] = hi
    xl_ref[...] = lo


def rest_kernel(norm_scale, r_ref, w_ref, xh_ref, xl_ref, phl_ref, t_ref, rs_ref, ws_ref, out_hbm, obuf, sem, tiles=8):
    size = ROWS_OWN * X_DIM // tiles

    def put(i):
        return pltpu.make_async_copy(obuf.at[i], out_hbm.at[pl.ds(i * size, size), :], sem.at[i])

    for i in range(tiles):
        rows = slice(i * size, (i + 1) * size)
        ph, pl_ = phl_ref[rows, 0:NB], phl_ref[rows, NB : 2 * NB]
        xh = xh_ref[...]
        q = jnp.dot(ph, xh, preferred_element_type=F32) + jnp.dot(pl_, xh, preferred_element_type=F32)
        q = q + jnp.dot(ph, xl_ref[...], preferred_element_type=F32)
        obuf[i] = t_ref[rows, :] - q
        put(i).start()
    rs_ref[...] = r_ref[...] * norm_scale
    ws_ref[...] = w_ref[...] * norm_scale
    for i in range(tiles):
        put(i).wait()


def body(panel_block, trailing):
    total_rows = panel_block.shape[0] * lax.axis_size("row") * lax.axis_size("col")
    norm_scale = 1.0 / math.sqrt(total_rows)
    rows = trailing.shape[0]
    vm = pl.BlockSpec(memory_space=pltpu.VMEM)
    anym = pl.BlockSpec(memory_space=pl.ANY)

    def out(shape, dtype):
        return jax.ShapeDtypeStruct(shape, dtype)

    parts = pl.pallas_call(
        main_kernel,
        out_shape=[
            out((NB, NB), F32), out((NB, COLS_OWN), F32), out((NB, COLS_OWN), BF16), out((NB, COLS_OWN), BF16),
            out((rows, 2 * NB), BF16), out((rows, COLS_OWN), F32),
        ],
        in_specs=[pl.BlockSpec(memory_space=pltpu.HBM)] * 2,
        out_specs=[vm] * 6,
        scratch_shapes=[
            pltpu.VMEM((X_DIM, ROWS_OWN, NB), F32),
            pltpu.VMEM((2, rows, COLS_OWN), BF16),
            pltpu.VMEM((16, 8, NB), F32),
            pltpu.VMEM((15, 8, NB), F32),
            pltpu.VMEM((16, 8, NB), F32),
            pltpu.VMEM((8, NB), F32),
            pltpu.VMEM((16, 8, NB), F32),
            pltpu.VMEM((NB, NB), F32),
            pltpu.VMEM((64, 8, NB), F32),
            pltpu.VMEM((32, 8, NB), F32),
            pltpu.VMEM((32, 8, NB), F32),
            pltpu.VMEM((31, 8, NB), F32),
            pltpu.VMEM((64, 8, NB), F32),
            pltpu.SemaphoreType.DMA((5,)),
            pltpu.SemaphoreType.DMA((6,)),
            pltpu.SemaphoreType.DMA((6,)),
            pltpu.SemaphoreType.DMA((7,)),
            pltpu.SemaphoreType.DMA((7,)),
        ],
        compiler_params=pltpu.CompilerParams(collective_id=0, has_side_effects=True, vmem_limit_bytes=40 << 20),
    )(panel_block, trailing)
    return pl.pallas_call(
        lambda *refs: rest_kernel(norm_scale, *refs),
        out_shape=[out((NB, NB), F32), out((NB, COLS_OWN), F32), out((rows, COLS_OWN), F32)],
        in_specs=[vm] * 6,
        out_specs=[vm, vm, anym],
        scratch_shapes=[pltpu.VMEM((8, rows // 8, COLS_OWN), F32), pltpu.SemaphoreType.DMA((8,))],
        compiler_params=pltpu.CompilerParams(vmem_limit_bytes=40 << 20),
    )(*parts)


def solution(mesh):
    in_specs = (P(("row", "col"), None), P("row", "col"))
    out_specs = (P(), P(None, "col"), P("row", "col"))
    return jax.shard_map(body, mesh=mesh, in_specs=in_specs, out_specs=out_specs, check_vma=False)
```

time: 1180 us -> 53.5 us (0.05)
  matrix products: 424 us -> 0 us
  waiting for transfers between devices: 419 us -> 0 us
  other arithmetic: 214 us -> 0 us
  loops' own time: 95.4 us -> 0 us
  Pallas kernels: 0 us -> 49.6 us
  between operations: 15.5 us -> 0.65 us
    dot_general x388 -> x0, matrix products: 424 us -> none  [the longest x128 209 us: column_step(): column = jnp.dot(remaining, picker, precision=lax.Precision.HIGHEST)]
    psum x2 -> x0, waiting for transfers between devices: 418 us -> none  [the longest x1 247 us: body(): gram = lax.psum(local_gram, ('row', 'col'))]
    add x256 -> x0, other arithmetic: 211 us -> none  [the longest x128 198 us: column_step(): lower = lower + column[:, None] * picker[None, :]]
    another operation x2 -> x0, loops' own time: 95.4 us -> none  [the longest x1 91.4 us: upper_factor(): remaining, lower = lax.fori_loop(0, width, column_step, start)]
    pallas_call x0 -> x2, Pallas kernels: none -> 49.6 us  [the longest x1 46.3 us: body(): pl.pallas_call(main_kernel, out_shape=[out((NB, NB), F32), out((NB, COLS_...]
  transfers between devices with their start and end apart: 3 -> 0, of which waited for: 2 -> 0; matrix products, arithmetic and copies ran while one was open for 53% -> 0% of each run, Pallas kernels for 0% -> 0%
where the time goes in v1:
time: 53.5 us; the launch traced here: 53.4 us
  Pallas kernels  49.6 us (93%)
  local copies, waits for them, and re-layouts  3.13 us (6%)
  between operations  0.65 us (1%)
    pallas_call x1, Pallas kernels, body(): pl.pallas_call(main_kernel, out_shape=[out((NB, NB), F32), out((NB, COLS_...  46.3 us
    pallas_call x1, Pallas kernels, body(): pl.pallas_call(lambda *refs: rest_kernel(norm_scale, *refs), out_shape=[o...  3.36 us
    unnamed x4, local copies, waits for them, and re-layouts  3.13 us

profile of v1, /device:TPU:1, one launch (start us, length us, event | category | flops | bytes accessed | tf_op | source)
XLA Modules:
  0.0 53.4 jit_solution(1489011410719986273)
XLA Ops:
  0.6 0.0 copy-start
  0.6 2.2 %copy-done = f32[2048,512]{1,0:T(8,128)S(1)} copy-done((f32[2048,512]{1,0:T(8,128)S(1)}, f32[2048,512]{1,0:T(8,128)}, u32[]{:S(2)}) %copy-start) | copy-done | bytes 4194328
  2.8 0.0 copy-start.1
  2.8 0.9 %copy-done.1 = f32[512,128]{1,0:T(8,128)S(1)} copy-done((f32[512,128]{1,0:T(8,128)S(1)}, f32[512,128]{1,0:T(8,128)}, u32[]{:S(2)}) %copy-start.1) | copy-done | bytes 262168
  3.8 46.3 %shard_map.49 = (f32[128,128]{1,0:T(8,128)S(1)}, f32[128,512]{1,0:T(8,128)S(1)}, bf16[128,512]{1,0:T(8,128)(2,1)S(1)}, bf16[128,512]{1,0:T(8,128)(2,1)S(1)}, bf1...) custom-call(f32[512,128]{1,0:T(8,128)S(1)} %copy-done.1, f32[2048,512]{1,0:T(8,128)S(1)} %copy-done), custom_call_target="tpu_custom_call" | custom-call | tf_op jit(solution)/shard_map/pallas_call | solution.py:339
  50.0 3.4 %shard_map.50 = (f32[128,128]{1,0:T(8,128)}, f32[128,512]{1,0:T(8,128)}, f32[2048,512]{1,0:T(8,128)}) custom-call(f32[128,128]{1,0:T(8,128)S(1)} %get-tuple-element.9.refs_0_, f32[128,512]{1,0:T(8,128)S(1)} %get-tuple-element.10.refs_1_, bf16[128,512]{1,0:T(8,128)(2,1)S(1)} %get-tuple-element.11.refs_2_, bf16[128,512]{1,0:T(8,128)(2,1)S(1)} %get-tuple-element.12.refs_3_, ...), custom_call_target="tpu_custom_call" | custom-call | tf_op jit(solution)/shard_map/pallas_call | solution.py:369
Async XLA Ops:
  0.6 2.2 %copy-start = (f32[2048,512]{1,0:T(8,128)S(1)}, f32[2048,512]{1,0:T(8,128)}, u32[]{:S(2)}) copy-start(f32[2048,512]{1,0:T(8,128)} %t_hbm.1) | copy-start | bytes 12582916
  2.8 0.9 %copy-start.1 = (f32[512,128]{1,0:T(8,128)S(1)}, f32[512,128]{1,0:T(8,128)}, u32[]{:S(2)}) copy-start(f32[512,128]{1,0:T(8,128)} %p_hbm.1) | copy-start | bytes 786436

commit v2 on v1

--- a/solution.py
+++ b/solution.py
@@ -97,8 +97,8 @@
 def main_kernel(
     p_hbm, t_hbm,
     r_ref, w_ref, xh_ref, xl_ref, phl_ref, t_ref,
-    pg, thl, gbuf, abuf, bbuf, tile, gfull, y_ref, sbuf, cbuf, sred, rbuf, sfull,
-    load_sem, gsend, grecv, esend, erecv,
+    pg, thl, gbuf, abuf, bbuf, gfull, y_ref, sbuf, cbuf, sred, rbuf, sfull,
+    load_sem, gsend, grecv, esend, erecv, know_sem,
 ):
     row = lax.axis_index("row")
     col = lax.axis_index("col")
@@ -113,18 +113,26 @@
 
     sibling = (row + 1 - 2 * core, col)
 
+    def hops(n, d):
+        return min(d, n - d)
+
+    def far_first(n, m):
+        pairs = [(i, j) for i in range(n) for j in range(m) if i or j]
+        return sorted(pairs, key=lambda p: -hops(n, p[0]) - hops(m, p[1]))
+
+    def chip_peer(d):
+        z_, y_ = lax.rem(z + d[0], Z_DIM), lax.rem(y + d[1], Y_DIM)
+        return z_ * Y_DIM + y_, (device(z_, y_, core), col)
+
     def zc_peer(d):
-        q = lax.rem(z * 2 + core + d, 2 * Z_DIM)
-        return q, (device(lax.div(q, 2), y, lax.rem(q, 2)), col)
+        z_ = lax.rem(z + d[0], Z_DIM)
+        return (device(z_, y, 1 - core if d[1] else core), col)
 
     def yx_peer(d):
-        s = lax.rem(y * X_DIM + col + d, Y_DIM * X_DIM)
-        return s, (device(z, lax.div(s, X_DIM), core), lax.rem(s, X_DIM))
-
-    def chip_peer(d):
-        m = lax.rem(chip + d, CHIPS)
-        return m, (m * 2 + core, col)
-
+        y_, x_ = lax.rem(y + d[0], Y_DIM), lax.rem(col + d[1], X_DIM)
+        return y_ * X_DIM + x_, (device(z, y_, core), x_)
+
+    n_zc, n_yx = 2 * Z_DIM - 1, Y_DIM * X_DIM - 1
     me_q = z * 2 + core
     me_s = y * X_DIM + col
 
@@ -152,27 +160,28 @@
 
         lax.fori_loop(lo, hi, step, 0)
 
-    each(1, CHIPS, lambda d: greet(chip_peer(d)[1]))
-    each(0, Z_DIM, lambda d: greet((device(d, y, 1 - core), col)))
-    each(1, X_DIM, lambda dx: each(0, Y_DIM, lambda d: greet((device(z, d, core), lax.rem(col + dx, X_DIM)))))
+    def greet_z(d):
+        z_ = lax.rem(z + d, Z_DIM)
+        greet((device(z_, y, core), col))
+        greet((device(z_, y, 1 - core), col))
+
+    each(1, 3, greet_z)
+    each(Z_DIM - 2, Z_DIM, greet_z)
+    greet(sibling)
+    each(1, X_DIM, lambda d: greet((row, lax.rem(col + d, X_DIM))))
+    each(1, Y_DIM, lambda d: greet((device(z, lax.rem(y + d, Y_DIM), core), col)))
 
     load_p().wait()
-    own = pg[col]
-    gram = inner(own, own, HIGHEST)
-    gbuf[...] = gram.reshape(NB // 8, 8, NB)
-    pl.semaphore_wait(barrier, CHIPS - 1 + Z_DIM + (X_DIM - 1) * Y_DIM)
+    pl.semaphore_wait(barrier, 9 + X_DIM - 1 + Y_DIM - 1)
+
+    def introduce(peer, k=0):
+        pl.semaphore_signal(know_sem.at[k], inc=1, device_id=peer, device_id_type=MESH)
 
     def remote(src, dst, send, recv, peer):
         return pltpu.make_async_remote_copy(
             src_ref=src, dst_ref=dst, send_sem=send, recv_sem=recv, device_id=peer, device_id_type=MESH
         )
 
-    def send_a(d):
-        q, peer = zc_peer(d)
-        remote(gbuf.at[q], abuf.at[d - 1], esend.at[0], erecv.at[0], peer).start()
-
-    each(1, 2 * Z_DIM, send_a)
-
     top, bottom = pl.ds(0, HALF), pl.ds(HALF, HALF)
 
     def ring(k, block, part, to):
@@ -182,6 +191,21 @@
     ring(1, col, bottom, left).start()
     ring(2, col, bottom, right).start()
     ring(3, col, top, left).start()
+
+    introduce((device(lax.rem(z + 2, Z_DIM), y, core), col))
+    introduce((device(lax.rem(z + Z_DIM - 2, Z_DIM), y, core), col))
+    each(1, X_DIM, lambda d: introduce((row, lax.rem(col + d, X_DIM))))
+
+    own = pg[col]
+    gram = inner(own, own, HIGHEST)
+    gbuf[...] = gram.reshape(NB // 8, 8, NB)
+
+    pl.semaphore_wait(know_sem.at[0], 2 + X_DIM - 1)
+    each(1, Y_DIM, lambda d: introduce((device(z, lax.rem(y + d, Y_DIM), core), col), 1))
+
+    for k, d in enumerate(far_first(Y_DIM, X_DIM)):
+        t, peer = yx_peer(d)
+        remote(gbuf.at[t], abuf.at[k], esend.at[0], erecv.at[0], peer).start()
 
     def split_t(k, b):
         load_t(b, k).wait()
@@ -211,47 +235,26 @@
     def sent(k, buf):
         remote(buf, buf, esend.at[k], erecv.at[k], sibling).wait_send()
 
-    n_zc, n_yx = 2 * Z_DIM - 1, Y_DIM * X_DIM - 1
-    received(0, abuf)
-    bbuf[me_s] = gbuf[me_q] + jnp.sum(abuf[...], axis=0)
-
-    def send_b(d):
-        _, peer = yx_peer(d)
-        remote(bbuf.at[me_s], bbuf.at[me_s], esend.at[1], erecv.at[1], peer).start()
-
-    each(1, n_yx + 1, send_b)
-
-    split_t(1, order[1])
-    split_t(2, order[2])
-
     ring(0, left, top, right).wait_recv()
     ring(4, left, top, right).start()
     ring(1, right, bottom, left).wait_recv()
     ring(5, right, bottom, left).start()
 
-    received(1, bbuf.at[pl.ds(0, n_yx)])
-    gfull[me_q] = jnp.sum(bbuf[...], axis=0)
-
-    def send_c(d):
-        _, peer = zc_peer(d)
-        remote(gfull.at[me_q], gfull.at[me_q], esend.at[2], erecv.at[2], peer).start()
-
-    each(1, n_zc + 1, send_c)
-
+    split_t(1, order[1])
+    split_t(2, order[2])
     split_t(3, order[3])
+
+    received(0, abuf)
+    bbuf[me_q] = gbuf[me_s] + jnp.sum(abuf[...], axis=0)
+
+    for d in far_first(Z_DIM, 2):
+        remote(bbuf.at[me_q], bbuf.at[me_q], esend.at[1], erecv.at[1], zc_peer(d)).start()
+
     ring(2, left, bottom, right).wait_recv()
     product(left)
     ring(3, right, top, left).wait_recv()
     product(right)
 
-    received(2, gfull.at[pl.ds(0, n_zc)])
-    steps = factor_steps([gfull[i] for i in range(NB // 8)], r_ref, y_ref)
-
-    def factor(count):
-        for _ in range(count):
-            next(steps)
-
-    factor(3)
     ring(4, across, top, right).wait_recv()
     ring(5, across, bottom, left).wait_recv()
     product(across)
@@ -260,29 +263,35 @@
     other = pl.ds(pl.multiple_of((1 - core) * CHIPS, CHIPS), CHIPS)
     swap = remote(sbuf.at[other], cbuf, esend.at[3], erecv.at[3], sibling)
     swap.start()
-    factor(3)
+
     swap.wait_recv()
     sred[...] = sbuf[mine] + cbuf[...]
 
-    def send_rs(d):
+    pl.semaphore_wait(know_sem.at[1], Y_DIM - 1)
+    for k, d in enumerate(far_first(Z_DIM, Y_DIM)):
         m, peer = chip_peer(d)
-        remote(sred.at[m], rbuf.at[d - 1], esend.at[4], erecv.at[4], peer).start()
-
-    each(1, CHIPS, send_rs)
-    factor(6)
+        remote(sred.at[m], rbuf.at[k], esend.at[4], erecv.at[4], peer).start()
+
+    received(1, bbuf.at[pl.ds(0, n_zc)])
+    gfull[me_s] = jnp.sum(bbuf[...], axis=0)
+
+    for d in far_first(Y_DIM, X_DIM):
+        remote(gfull.at[me_s], gfull.at[me_s], esend.at[2], erecv.at[2], yx_peer(d)[1]).start()
+
     received(4, rbuf)
     slot = core * CHIPS + chip
     sfull[slot] = sred[chip] + jnp.sum(rbuf[...], axis=0)
 
-    def send_ag(d):
-        _, peer = chip_peer(d)
-        remote(sfull.at[slot], sfull.at[slot], esend.at[5], erecv.at[5], peer).start()
-
-    each(1, CHIPS, send_ag)
-    factor(4)
-    received(5, sfull.at[pl.ds(0, CHIPS - 1)])
-    last = remote(sfull.at[mine], sfull.at[mine], esend.at[6], erecv.at[6], sibling)
-    last.start()
+    for d in far_first(Z_DIM, Y_DIM):
+        remote(sfull.at[slot], sfull.at[slot], esend.at[5], erecv.at[5], chip_peer(d)[1]).start()
+    received(2, gfull.at[pl.ds(0, n_yx)])
+    steps = factor_steps([gfull[i] for i in range(NB // 8)], r_ref, y_ref)
+
+    def factor(count):
+        for _ in range(count):
+            next(steps)
+
+    factor(16)
 
     for k, block, part, to in (
         (0, col, top, right), (1, col, bottom, left), (2, col, bottom, right),
@@ -290,38 +299,52 @@
     ):
         ring(k, block, part, to).wait_send()
     sent(0, abuf)
-    sent(1, bbuf.at[pl.ds(0, n_yx)])
-    sent(2, gfull.at[pl.ds(0, n_zc)])
+    sent(1, bbuf.at[pl.ds(0, n_zc)])
+    sent(2, gfull.at[pl.ds(0, n_yx)])
     swap.wait_send()
     sent(4, rbuf)
+
+    inv_t = y_ref[...]
+    both = jnp.concatenate([inv_t, inner(inv_t, inv_t, HIGHEST)], axis=0)
+
+    def finish(h):
+        tiles = [sfull[pl.ds(pl.multiple_of(h * CHIPS + 16 * j, 16), 16)].reshape(NB, NB) for j in range(2)]
+        wx = jnp.dot(both, jnp.concatenate(tiles, axis=1), precision=HIGHEST, preferred_element_type=F32)
+        at = pl.ds(pl.multiple_of(h * (COLS_OWN // 2), COLS_OWN // 2), COLS_OWN // 2)
+        w_ref[:, at] = wx[:NB]
+        hi, lo = split(wx[NB:])
+        xh_ref[0:NB, at] = hi
+        xh_ref[NB : 2 * NB, at] = hi
+        xl_ref[:, at] = lo
+
+    received(5, sfull.at[pl.ds(0, CHIPS - 1)])
+    last = remote(sfull.at[mine], sfull.at[mine], esend.at[6], erecv.at[6], sibling)
+    last.start()
+    finish(core)
     sent(5, sfull.at[pl.ds(0, CHIPS - 1)])
-
     last.wait()
-    s = jnp.concatenate([sfull[16 * j : 16 * (j + 1)].reshape(NB, NB) for j in range(4)], axis=1)
-    inv_t = y_ref[...]
-    w = jnp.dot(inv_t, s, precision=HIGHEST, preferred_element_type=F32)
-    w_ref[...] = w
-    hi, lo = split(inner(inv_t, w, HIGHEST))
-    xh_ref[...] = hi
-    xl_ref[...] = lo
-
-
-def rest_kernel(norm_scale, r_ref, w_ref, xh_ref, xl_ref, phl_ref, t_ref, rs_ref, ws_ref, out_hbm, obuf, sem, tiles=8):
+    finish(1 - core)
+
+
+def rest_kernel(norm_scale, r_ref, w_ref, xh_ref, xl_ref, phl_ref, t_ref, rs_hbm, ws_hbm, out_hbm, rs, ws, obuf, sem, tiles=8):
     size = ROWS_OWN * X_DIM // tiles
 
     def put(i):
         return pltpu.make_async_copy(obuf.at[i], out_hbm.at[pl.ds(i * size, size), :], sem.at[i])
 
+    scaled = [pltpu.make_async_copy(rs, rs_hbm, sem.at[tiles]), pltpu.make_async_copy(ws, ws_hbm, sem.at[tiles + 1])]
+    rs[...] = r_ref[...] * norm_scale
+    ws[...] = w_ref[...] * norm_scale
+    for copy in scaled:
+        copy.start()
     for i in range(tiles):
         rows = slice(i * size, (i + 1) * size)
-        ph, pl_ = phl_ref[rows, 0:NB], phl_ref[rows, NB : 2 * NB]
-        xh = xh_ref[...]
-        q = jnp.dot(ph, xh, preferred_element_type=F32) + jnp.dot(pl_, xh, preferred_element_type=F32)
-        q = q + jnp.dot(ph, xl_ref[...], preferred_element_type=F32)
+        q = jnp.dot(phl_ref[rows, :], xh_ref[...], preferred_element_type=F32)
+        q = q + jnp.dot(phl_ref[rows, 0:NB], xl_ref[...], preferred_element_type=F32)
         obuf[i] = t_ref[rows, :] - q
         put(i).start()
-    rs_ref[...] = r_ref[...] * norm_scale
-    ws_ref[...] = w_ref[...] * norm_scale
+    for copy in scaled:
+        copy.wait()
     for i in range(tiles):
         put(i).wait()
 
@@ -339,7 +362,7 @@
     parts = pl.pallas_call(
         main_kernel,
         out_shape=[
-            out((NB, NB), F32), out((NB, COLS_OWN), F32), out((NB, COLS_OWN), BF16), out((NB, COLS_OWN), BF16),
+            out((NB, NB), F32), out((NB, COLS_OWN), F32), out((2 * NB, COLS_OWN), BF16), out((NB, COLS_OWN), BF16),
             out((rows, 2 * NB), BF16), out((rows, COLS_OWN), F32),
         ],
         in_specs=[pl.BlockSpec(memory_space=pltpu.HBM)] * 2,
@@ -350,7 +373,6 @@
             pltpu.VMEM((16, 8, NB), F32),
             pltpu.VMEM((15, 8, NB), F32),
             pltpu.VMEM((16, 8, NB), F32),
-            pltpu.VMEM((8, NB), F32),
             pltpu.VMEM((16, 8, NB), F32),
             pltpu.VMEM((NB, NB), F32),
             pltpu.VMEM((64, 8, NB), F32),
@@ -363,15 +385,19 @@
             pltpu.SemaphoreType.DMA((6,)),
             pltpu.SemaphoreType.DMA((7,)),
             pltpu.SemaphoreType.DMA((7,)),
+            pltpu.SemaphoreType.REGULAR((2,)),
         ],
         compiler_params=pltpu.CompilerParams(collective_id=0, has_side_effects=True, vmem_limit_bytes=40 << 20),
-    )(panel_block, trailing)
+    )(*(pltpu.with_memory_space_constraint(a, pltpu.HBM) for a in (panel_block, trailing)))
     return pl.pallas_call(
         lambda *refs: rest_kernel(norm_scale, *refs),
         out_shape=[out((NB, NB), F32), out((NB, COLS_OWN), F32), out((rows, COLS_OWN), F32)],
         in_specs=[vm] * 6,
-        out_specs=[vm, vm, anym],
-        scratch_shapes=[pltpu.VMEM((8, rows // 8, COLS_OWN), F32), pltpu.SemaphoreType.DMA((8,))],
+        out_specs=[anym] * 3,
+        scratch_shapes=[
+            pltpu.VMEM((NB, NB), F32), pltpu.VMEM((NB, COLS_OWN), F32),
+            pltpu.VMEM((8, rows // 8, COLS_OWN), F32), pltpu.SemaphoreType.DMA((10,)),
+        ],
         compiler_params=pltpu.CompilerParams(vmem_limit_bytes=40 << 20),
     )(*parts)
 

time: 53.5 us -> 40.4 us (0.76)
  Pallas kernels: 49.6 us -> 39.6 us
  local copies, waits for them, and re-layouts: 3.13 us -> 0 us
    pallas_call x1, Pallas kernels: 46.3 us -> 37.2 us  [body(): pl.pallas_call(main_kernel, out_shape=[out((NB, NB), F32), out((NB, COLS_...]
    unnamed x4 -> x0, local copies, waits for them, and re-layouts: 3.13 us -> none
    pallas_call x1, Pallas kernels: 3.36 us -> 2.49 us  [body(): pl.pallas_call(lambda *refs: rest_kernel(norm_scale, *refs), out_shape=[o...]
where the time goes in v2:
time: 40.4 us; the launch traced here: 40.3 us
  Pallas kernels  39.6 us (98%)
  between operations  0.64 us (2%)
    pallas_call x1, Pallas kernels, body(): pl.pallas_call(main_kernel, out_shape=[out((NB, NB), F32), out((NB, COLS_...  37.2 us
    pallas_call x1, Pallas kernels, body(): pl.pallas_call(lambda *refs: rest_kernel(norm_scale, *refs), out_shape=[o...  2.49 us

profile of v2, /device:TPU:1, one launch (start us, length us, event | category | flops | bytes accessed | tf_op | source)
XLA Modules:
  0.0 40.3 jit_solution(3688151105893142648)
XLA Ops:
  0.6 37.2 %shard_map.49 = (f32[128,128]{1,0:T(8,128)S(1)}, f32[128,512]{1,0:T(8,128)S(1)}, bf16[256,512]{1,0:T(8,128)(2,1)S(1)}, bf16[128,512]{1,0:T(8,128)(2,1)S(1)}, bf1...) custom-call(f32[512,128]{1,0:T(8,128)} %p_hbm.1, f32[2048,512]{1,0:T(8,128)} %t_hbm.1), custom_call_target="tpu_custom_call" | custom-call | tf_op jit(solution)/shard_map/pallas_call | solution.py:362
  37.8 2.5 %shard_map.50 = (f32[128,128]{1,0:T(8,128)}, f32[128,512]{1,0:T(8,128)}, f32[2048,512]{1,0:T(8,128)}) custom-call(f32[128,128]{1,0:T(8,128)S(1)} %get-tuple-element.9.refs_0_, f32[128,512]{1,0:T(8,128)S(1)} %get-tuple-element.10.refs_1_, bf16[256,512]{1,0:T(8,128)(2,1)S(1)} %get-tuple-element.11.refs_2_, bf16[128,512]{1,0:T(8,128)(2,1)S(1)} %get-tuple-element.12.refs_3_, ...), custom_call_target="tpu_custom_call" | custom-call | tf_op jit(solution)/shard_map/pallas_call | solution.py:392

commit v3 on v2

--- a/solution.py
+++ b/solution.py
@@ -19,11 +19,6 @@
 HALF = ROWS_OWN // 2
 
 
-def reciprocal(p):
-    r = pl.reciprocal(p, approx=True)
-    return r * (2.0 - p * r)
-
-
 def lane_spread(v, c):
     return jnp.broadcast_to(v[:, c : c + 1], (8, NB))
 
@@ -32,7 +27,7 @@
     return jnp.broadcast_to(v[j : j + 1, :], (8, NB))
 
 
-def factor_steps(g, r_ref, y_ref):
+def factor_gram(g, r_ref, y_ref):
     sub = lax.broadcasted_iota(jnp.int32, (8, NB), 0)
     lane = lax.broadcasted_iota(jnp.int32, (8, NB), 1)
     n = NB // 8
@@ -43,26 +38,28 @@
         diag = [lane_spread(v, 8 * k + j) for j in range(8)]
         more = k + 1 < n
         if more:
-            diag2 = [lane_spread(left[k + 1], 8 * k + j) for j in range(8)]
             v2, w2 = left[k + 1], right[k + 1]
+            diag2 = [lane_spread(v2, 8 * k + j) for j in range(8)]
         pivots = jnp.ones((8, NB), F32)
+        p = row_spread(diag[0], 0)
         for j in range(8):
-            p = row_spread(diag[j], j)
-            r = reciprocal(p)
-            m = jnp.where(sub > j, diag[j] * r, 0.0)
+            r0 = pltpu.reciprocal(p, approx=True)
+            e = 2.0 - p * r0
+            r = r0 * e
+            pivots = jnp.where(sub == j, p, pivots)
+            rows = [row_spread(diag[jj], j) for jj in range(j + 1, 8)]
+            if rows:
+                p = row_spread(diag[j + 1], j + 1) - (rows[0] * rows[0] * r0) * e
+            m = jnp.where(sub > j, diag[j], 0.0) * r
             vj, wj = row_spread(v, j), row_spread(w, j)
-            v = v - m * vj
-            w = w - m * wj
+            v, w = v - m * vj, w - m * wj
             if more:
                 m2 = diag2[j] * r
-                v2 = v2 - m2 * vj
-                w2 = w2 - m2 * wj
-            for jj in range(j + 1, 8):
-                c = row_spread(diag[jj], j)
-                diag[jj] = diag[jj] - m * c
+                v2, w2 = v2 - m2 * vj, w2 - m2 * wj
+            for jj, row in zip(range(j + 1, 8), rows):
+                diag[jj] = diag[jj] - m * row
                 if more:
-                    diag2[jj] = diag2[jj] - m2 * c
-            pivots = jnp.where(sub == j, p, pivots)
+                    diag2[jj] = diag2[jj] - m2 * row
         scale = lax.rsqrt(pivots)
         u = jnp.where(lane >= 8 * k + sub, v * scale, 0.0)
         z = w * scale
@@ -71,18 +68,19 @@
         if more:
             left[k + 1], right[k + 1] = v2, w2
         if k + 2 < n:
-            ut = u.T
-            us = [row_spread(u, j) for j in range(8)]
-            zs = [row_spread(z, j) for j in range(8)]
+            uz = jnp.concatenate([u, z], axis=1)
+            high = uz.astype(BF16).astype(F32)
+            mid = (uz - high).astype(BF16).astype(F32)
+            low = uz - high - mid
+            one = [high, high, mid, high, mid, low]
+            two = [high, mid, high, low, mid, high]
+            drop = inner(
+                jnp.concatenate([q[:, :NB] for q in one], axis=0).astype(BF16),
+                jnp.concatenate(two, axis=0).astype(BF16),
+            )
             for i in range(k + 2, n):
-                t = ut[8 * i : 8 * i + 8, :]
-                a, b = left[i], right[i]
-                for j in range(8):
-                    tj = jnp.broadcast_to(t[:, j : j + 1], (8, NB))
-                    a = a - tj * us[j]
-                    b = b - tj * zs[j]
-                left[i], right[i] = a, b
-        yield
+                left[i] = left[i] - drop[8 * i : 8 * i + 8, :NB]
+                right[i] = right[i] - drop[8 * i : 8 * i + 8, NB:]
 
 
 def split(x):
@@ -160,19 +158,18 @@
 
         lax.fori_loop(lo, hi, step, 0)
 
-    def greet_z(d):
-        z_ = lax.rem(z + d, Z_DIM)
-        greet((device(z_, y, core), col))
-        greet((device(z_, y, 1 - core), col))
-
-    each(1, 3, greet_z)
-    each(Z_DIM - 2, Z_DIM, greet_z)
+    z_next, z_prev = (lax.rem(z + d, Z_DIM) for d in (1, Z_DIM - 1))
+    y_next, y_prev = (lax.rem(y + d, Y_DIM) for d in (1, Y_DIM - 1))
+    near = (
+        (row, right), (row, left), (device(z, y_next, core), col), (device(z, y_prev, core), col),
+        (device(z_next, y, core), col), (device(z_prev, y, core), col),
+    )
+    for peer in near:
+        greet(peer)
     greet(sibling)
-    each(1, X_DIM, lambda d: greet((row, lax.rem(col + d, X_DIM))))
-    each(1, Y_DIM, lambda d: greet((device(z, lax.rem(y + d, Y_DIM), core), col)))
 
     load_p().wait()
-    pl.semaphore_wait(barrier, 9 + X_DIM - 1 + Y_DIM - 1)
+    pl.semaphore_wait(barrier, 7)
 
     def introduce(peer, k=0):
         pl.semaphore_signal(know_sem.at[k], inc=1, device_id=peer, device_id_type=MESH)
@@ -185,27 +182,26 @@
     top, bottom = pl.ds(0, HALF), pl.ds(HALF, HALF)
 
     def ring(k, block, part, to):
-        return remote(pg.at[block, part, :], pg.at[block, part, :], gsend.at[k], grecv.at[k], (row, to))
+        src = pg.at[block, part, :]
+        return remote(src, pg.at[block, part, :], gsend.at[k], grecv.at[k], (row, to))
 
     ring(0, col, top, right).start()
     ring(1, col, bottom, left).start()
     ring(2, col, bottom, right).start()
     ring(3, col, top, left).start()
 
-    introduce((device(lax.rem(z + 2, Z_DIM), y, core), col))
-    introduce((device(lax.rem(z + Z_DIM - 2, Z_DIM), y, core), col))
-    each(1, X_DIM, lambda d: introduce((row, lax.rem(col + d, X_DIM))))
+    for peer in near:
+        introduce(peer)
 
     own = pg[col]
     gram = inner(own, own, HIGHEST)
     gbuf[...] = gram.reshape(NB // 8, 8, NB)
 
-    pl.semaphore_wait(know_sem.at[0], 2 + X_DIM - 1)
-    each(1, Y_DIM, lambda d: introduce((device(z, lax.rem(y + d, Y_DIM), core), col), 1))
-
-    for k, d in enumerate(far_first(Y_DIM, X_DIM)):
-        t, peer = yx_peer(d)
-        remote(gbuf.at[t], abuf.at[k], esend.at[0], erecv.at[0], peer).start()
+    pl.semaphore_wait(know_sem.at[0], len(near))
+    introduce((device(lax.rem(z + 2, Z_DIM), y, core), col), 1)
+    introduce((device(lax.rem(z + Z_DIM - 2, Z_DIM), y, core), col), 1)
+    for to in (right, left, across):
+        introduce((row, to), 1)
 
     def split_t(k, b):
         load_t(b, k).wait()
@@ -214,20 +210,35 @@
         thl[0, rows, :] = hi
         thl[1, rows, :] = lo
 
-    def product(b, first=False):
-        rows = pl.ds(pl.multiple_of(b * ROWS_OWN, ROWS_OWN), ROWS_OWN)
+    def rows_of(b):
+        return pl.ds(pl.multiple_of(b * ROWS_OWN, ROWS_OWN), ROWS_OWN)
+
+    def split_p(b):
         hi, lo = split(pg[b])
-        phl_ref[rows, 0:NB] = hi
-        phl_ref[rows, NB : 2 * NB] = lo
-        th = thl[0, rows, :]
-        s = inner(hi, th) + inner(lo, th) + inner(hi, thl[1, rows, :])
-        for j in range(4):
+        phl_ref[rows_of(b), 0:NB] = hi
+        phl_ref[rows_of(b), NB : 2 * NB] = lo
+
+    def product(b, h, first=False):
+        at = pl.ds(pl.multiple_of(h * (COLS_OWN // 2), COLS_OWN // 2), COLS_OWN // 2)
+        hi, lo = phl_ref[rows_of(b), 0:NB], phl_ref[rows_of(b), NB : 2 * NB]
+        th = thl[0, rows_of(b), at]
+        s = inner(hi, th) + inner(lo, th) + inner(hi, thl[1, rows_of(b), at])
+        for j in range(2):
             t = s[:, NB * j : NB * (j + 1)].reshape(16, 8, NB)
-            at = slice(16 * j, 16 * (j + 1))
-            sbuf[at] = t if first else sbuf[at] + t
+            tiles = pl.ds(pl.multiple_of(h * CHIPS + 16 * j, 16), 16)
+            sbuf[tiles] = t if first else sbuf[tiles] + t
 
     split_t(0, order[0])
-    product(col, True)
+    split_p(col)
+    product(col, 0, True)
+    product(col, 1, True)
+    pl.semaphore_wait(know_sem.at[1], 2 + X_DIM - 1)
+    each(1, Y_DIM, lambda d: introduce((device(z, lax.rem(y + d, Y_DIM), core), col), 2))
+    introduce(sibling, 2)
+
+    for k, d in enumerate(far_first(Y_DIM, X_DIM)):
+        t, peer = yx_peer(d)
+        remote(gbuf.at[t], abuf.at[k], esend.at[0], erecv.at[0], peer).start()
 
     def received(k, buf):
         remote(buf, buf, esend.at[k], erecv.at[k], sibling).wait_recv()
@@ -247,27 +258,33 @@
     received(0, abuf)
     bbuf[me_q] = gbuf[me_s] + jnp.sum(abuf[...], axis=0)
 
+    pl.semaphore_wait(know_sem.at[2], Y_DIM)
+
     for d in far_first(Z_DIM, 2):
         remote(bbuf.at[me_q], bbuf.at[me_q], esend.at[1], erecv.at[1], zc_peer(d)).start()
 
     ring(2, left, bottom, right).wait_recv()
-    product(left)
+    split_p(left)
+    product(left, 0)
+    product(left, 1)
     ring(3, right, top, left).wait_recv()
-    product(right)
+    split_p(right)
+    product(right, 0)
+    product(right, 1)
 
     ring(4, across, top, right).wait_recv()
     ring(5, across, bottom, left).wait_recv()
-    product(across)
+    split_p(across)
+    product(across, 1 - core)
 
     mine = pl.ds(pl.multiple_of(core * CHIPS, CHIPS), CHIPS)
     other = pl.ds(pl.multiple_of((1 - core) * CHIPS, CHIPS), CHIPS)
     swap = remote(sbuf.at[other], cbuf, esend.at[3], erecv.at[3], sibling)
     swap.start()
-
+    product(across, core)
     swap.wait_recv()
     sred[...] = sbuf[mine] + cbuf[...]
 
-    pl.semaphore_wait(know_sem.at[1], Y_DIM - 1)
     for k, d in enumerate(far_first(Z_DIM, Y_DIM)):
         m, peer = chip_peer(d)
         remote(sred.at[m], rbuf.at[k], esend.at[4], erecv.at[4], peer).start()
@@ -285,13 +302,7 @@
     for d in far_first(Z_DIM, Y_DIM):
         remote(sfull.at[slot], sfull.at[slot], esend.at[5], erecv.at[5], chip_peer(d)[1]).start()
     received(2, gfull.at[pl.ds(0, n_yx)])
-    steps = factor_steps([gfull[i] for i in range(NB // 8)], r_ref, y_ref)
-
-    def factor(count):
-        for _ in range(count):
-            next(steps)
-
-    factor(16)
+    factor_gram([gfull[i] for i in range(NB // 8)], r_ref, y_ref)
 
     for k, block, part, to in (
         (0, col, top, right), (1, col, bottom, left), (2, col, bottom, right),
@@ -385,7 +396,7 @@
             pltpu.SemaphoreType.DMA((6,)),
             pltpu.SemaphoreType.DMA((7,)),
             pltpu.SemaphoreType.DMA((7,)),
-            pltpu.SemaphoreType.REGULAR((2,)),
+            pltpu.SemaphoreType.REGULAR((3,)),
         ],
         compiler_params=pltpu.CompilerParams(collective_id=0, has_side_effects=True, vmem_limit_bytes=40 << 20),
     )(*(pltpu.with_memory_space_constraint(a, pltpu.HBM) for a in (panel_block, trailing)))

time: 40.4 us -> 39.8 us (0.985)
  Pallas kernels: 39.6 us -> 39 us
    pallas_call x1, Pallas kernels: 37.2 us -> 36.6 us  [body(): pl.pallas_call(main_kernel, out_shape=[out((NB, NB), F32), out((NB, COLS_...]
where the time goes in v3:
time: 39.8 us; the launch traced here: 39.7 us
  Pallas kernels  39 us (98%)
  between operations  0.64 us (2%)
    pallas_call x1, Pallas kernels, body(): pl.pallas_call(main_kernel, out_shape=[out((NB, NB), F32), out((NB, COLS_...  36.6 us
    pallas_call x1, Pallas kernels, body(): pl.pallas_call(lambda *refs: rest_kernel(norm_scale, *refs), out_shape=[o...  2.49 us

profile of v3, /device:TPU:1, one launch (start us, length us, event | category | flops | bytes accessed | tf_op | source)
XLA Modules:
  0.0 39.7 jit_solution(14591870859649895520)
XLA Ops:
  0.6 36.6 %shard_map.49 = (f32[128,128]{1,0:T(8,128)S(1)}, f32[128,512]{1,0:T(8,128)S(1)}, bf16[256,512]{1,0:T(8,128)(2,1)S(1)}, bf16[128,512]{1,0:T(8,128)(2,1)S(1)}, bf1...) custom-call(f32[512,128]{1,0:T(8,128)} %p_hbm.1, f32[2048,512]{1,0:T(8,128)} %t_hbm.1), custom_call_target="tpu_custom_call" | custom-call | tf_op jit(solution)/shard_map/pallas_call | solution.py:373
  37.2 2.5 %shard_map.50 = (f32[128,128]{1,0:T(8,128)}, f32[128,512]{1,0:T(8,128)}, f32[2048,512]{1,0:T(8,128)}) custom-call(f32[128,128]{1,0:T(8,128)S(1)} %get-tuple-element.9.refs_0_, f32[128,512]{1,0:T(8,128)S(1)} %get-tuple-element.10.refs_1_, bf16[256,512]{1,0:T(8,128)(2,1)S(1)} %get-tuple-element.11.refs_2_, bf16[128,512]{1,0:T(8,128)(2,1)S(1)} %get-tuple-element.12.refs_3_, ...), custom_call_target="tpu_custom_call" | custom-call | tf_op jit(solution)/shard_map/pallas_call | solution.py:403

commit v4 on v3

--- a/solution.py
+++ b/solution.py
@@ -232,24 +232,25 @@
     split_p(col)
     product(col, 0, True)
     product(col, 1, True)
-    pl.semaphore_wait(know_sem.at[1], 2 + X_DIM - 1)
-    each(1, Y_DIM, lambda d: introduce((device(z, lax.rem(y + d, Y_DIM), core), col), 2))
-    introduce(sibling, 2)
-
-    for k, d in enumerate(far_first(Y_DIM, X_DIM)):
-        t, peer = yx_peer(d)
-        remote(gbuf.at[t], abuf.at[k], esend.at[0], erecv.at[0], peer).start()
-
-    def received(k, buf):
-        remote(buf, buf, esend.at[k], erecv.at[k], sibling).wait_recv()
-
-    def sent(k, buf):
-        remote(buf, buf, esend.at[k], erecv.at[k], sibling).wait_send()
 
     ring(0, left, top, right).wait_recv()
     ring(4, left, top, right).start()
     ring(1, right, bottom, left).wait_recv()
     ring(5, right, bottom, left).start()
+
+    pl.semaphore_wait(know_sem.at[1], 2 + X_DIM - 1)
+    each(1, Y_DIM, lambda d: introduce((device(z, lax.rem(y + d, Y_DIM), core), col), 2))
+    introduce(sibling, 2)
+
+    for k, d in enumerate(far_first(Y_DIM, X_DIM)):
+        t, peer = yx_peer(d)
+        remote(gbuf.at[t], abuf.at[k], esend.at[0], erecv.at[0], peer).start()
+
+    def received(k, buf):
+        remote(buf, buf, esend.at[k], erecv.at[k], sibling).wait_recv()
+
+    def sent(k, buf):
+        remote(buf, buf, esend.at[k], erecv.at[k], sibling).wait_send()
 
     split_t(1, order[1])
     split_t(2, order[2])

time: 39.8 us -> 41.7 us (1.048)
  Pallas kernels: 39 us -> 41 us
    pallas_call x1, Pallas kernels: 36.6 us -> 38.5 us  [body(): pl.pallas_call(main_kernel, out_shape=[out((NB, NB), F32), out((NB, COLS_...]
where the time goes in v4:
time: 41.7 us
  Pallas kernels  41 us (98%)
  between operations  0.64 us (2%)
    pallas_call x1, Pallas kernels, body(): pl.pallas_call(main_kernel, out_shape=[out((NB, NB), F32), out((NB, COLS_...  38.5 us
    pallas_call x1, Pallas kernels, body(): pl.pallas_call(lambda *refs: rest_kernel(norm_scale, *refs), out_shape=[o...  2.49 us

profile of v4, /device:TPU:1, one launch (start us, length us, event | category | flops | bytes accessed | tf_op | source)
XLA Modules:
  0.0 41.7 jit_solution(17540779041317483852)
XLA Ops:
  0.6 38.5 %shard_map.49 = (f32[128,128]{1,0:T(8,128)S(1)}, f32[128,512]{1,0:T(8,128)S(1)}, bf16[256,512]{1,0:T(8,128)(2,1)S(1)}, bf16[128,512]{1,0:T(8,128)(2,1)S(1)}, bf1...) custom-call(f32[512,128]{1,0:T(8,128)} %p_hbm.1, f32[2048,512]{1,0:T(8,128)} %t_hbm.1), custom_call_target="tpu_custom_call" | custom-call | tf_op jit(solution)/shard_map/pallas_call | solution.py:374
  39.2 2.5 %shard_map.50 = (f32[128,128]{1,0:T(8,128)}, f32[128,512]{1,0:T(8,128)}, f32[2048,512]{1,0:T(8,128)}) custom-call(f32[128,128]{1,0:T(8,128)S(1)} %get-tuple-element.9.refs_0_, f32[128,512]{1,0:T(8,128)S(1)} %get-tuple-element.10.refs_1_, bf16[256,512]{1,0:T(8,128)(2,1)S(1)} %get-tuple-element.11.refs_2_, bf16[128,512]{1,0:T(8,128)(2,1)S(1)} %get-tuple-element.12.refs_3_, ...), custom_call_target="tpu_custom_call" | custom-call | tf_op jit(solution)/shard_map/pallas_call | solution.py:404

commit v5 on v3

--- a/solution.py
+++ b/solution.py
@@ -255,14 +255,6 @@
     split_t(2, order[2])
     split_t(3, order[3])
 
-    received(0, abuf)
-    bbuf[me_q] = gbuf[me_s] + jnp.sum(abuf[...], axis=0)
-
-    pl.semaphore_wait(know_sem.at[2], Y_DIM)
-
-    for d in far_first(Z_DIM, 2):
-        remote(bbuf.at[me_q], bbuf.at[me_q], esend.at[1], erecv.at[1], zc_peer(d)).start()
-
     ring(2, left, bottom, right).wait_recv()
     split_p(left)
     product(left, 0)
@@ -271,6 +263,14 @@
     split_p(right)
     product(right, 0)
     product(right, 1)
+
+    received(0, abuf)
+    bbuf[me_q] = gbuf[me_s] + jnp.sum(abuf[...], axis=0)
+
+    pl.semaphore_wait(know_sem.at[2], Y_DIM)
+
+    for d in far_first(Z_DIM, 2):
+        remote(bbuf.at[me_q], bbuf.at[me_q], esend.at[1], erecv.at[1], zc_peer(d)).start()
 
     ring(4, across, top, right).wait_recv()
     ring(5, across, bottom, left).wait_recv()

time: 39.8 us -> 39.5 us (level)
  no operation moved by 1% of the time
where the time goes in v5:
time: 39.5 us
  Pallas kernels  38.8 us (98%)
  between operations  0.64 us (2%)
    pallas_call x1, Pallas kernels, body(): pl.pallas_call(main_kernel, out_shape=[out((NB, NB), F32), out((NB, COLS_...  36.3 us
    pallas_call x1, Pallas kernels, body(): pl.pallas_call(lambda *refs: rest_kernel(norm_scale, *refs), out_shape=[o...  2.48 us

profile of v5, /device:TPU:1, one launch (start us, length us, event | category | flops | bytes accessed | tf_op | source)
XLA Modules:
  0.0 39.5 jit_solution(11807234741048426106)
XLA Ops:
  0.6 36.3 %shard_map.49 = (f32[128,128]{1,0:T(8,128)S(1)}, f32[128,512]{1,0:T(8,128)S(1)}, bf16[256,512]{1,0:T(8,128)(2,1)S(1)}, bf16[128,512]{1,0:T(8,128)(2,1)S(1)}, bf1...) custom-call(f32[512,128]{1,0:T(8,128)} %p_hbm.1, f32[2048,512]{1,0:T(8,128)} %t_hbm.1), custom_call_target="tpu_custom_call" | custom-call | tf_op jit(solution)/shard_map/pallas_call | solution.py:373
  37.0 2.5 %shard_map.50 = (f32[128,128]{1,0:T(8,128)}, f32[128,512]{1,0:T(8,128)}, f32[2048,512]{1,0:T(8,128)}) custom-call(f32[128,128]{1,0:T(8,128)S(1)} %get-tuple-element.9.refs_0_, f32[128,512]{1,0:T(8,128)S(1)} %get-tuple-element.10.refs_1_, bf16[256,512]{1,0:T(8,128)(2,1)S(1)} %get-tuple-element.11.refs_2_, bf16[128,512]{1,0:T(8,128)(2,1)S(1)} %get-tuple-element.12.refs_3_, ...), custom_call_target="tpu_custom_call" | custom-call | tf_op jit(solution)/shard_map/pallas_call | solution.py:403

commit v6 on v5

--- a/solution.py
+++ b/solution.py
@@ -142,10 +142,6 @@
         return pltpu.make_async_copy(t_hbm.at[rows, :], t_ref.at[rows, :], load_sem.at[k])
 
     load_p().start()
-    order = (col, left, right, across)
-    for k, b in enumerate(order):
-        load_t(b, k).start()
-
     barrier = pltpu.get_barrier_semaphore()
 
     def greet(peer):
@@ -167,6 +163,10 @@
     for peer in near:
         greet(peer)
     greet(sibling)
+
+    order = (col, left, right, across)
+    for k, b in enumerate(order):
+        load_t(b, k).start()
 
     load_p().wait()
     pl.semaphore_wait(barrier, 7)

time: 39.5 us -> 39.5 us (level)
  no operation moved by 1% of the time
where the time goes in v6:
time: 39.5 us
  Pallas kernels  38.8 us (98%)
  between operations  0.64 us (2%)
    pallas_call x1, Pallas kernels, body(): pl.pallas_call(main_kernel, out_shape=[out((NB, NB), F32), out((NB, COLS_...  36.3 us
    pallas_call x1, Pallas kernels, body(): pl.pallas_call(lambda *refs: rest_kernel(norm_scale, *refs), out_shape=[o...  2.49 us

profile of v6, /device:TPU:1, one launch (start us, length us, event | category | flops | bytes accessed | tf_op | source)
XLA Modules:
  0.0 39.5 jit_solution(4447218419254920850)
XLA Ops:
  0.6 36.3 %shard_map.49 = (f32[128,128]{1,0:T(8,128)S(1)}, f32[128,512]{1,0:T(8,128)S(1)}, bf16[256,512]{1,0:T(8,128)(2,1)S(1)}, bf16[128,512]{1,0:T(8,128)(2,1)S(1)}, bf1...) custom-call(f32[512,128]{1,0:T(8,128)} %p_hbm.1, f32[2048,512]{1,0:T(8,128)} %t_hbm.1), custom_call_target="tpu_custom_call" | custom-call | tf_op jit(solution)/shard_map/pallas_call | solution.py:373
  37.0 2.5 %shard_map.50 = (f32[128,128]{1,0:T(8,128)}, f32[128,512]{1,0:T(8,128)}, f32[2048,512]{1,0:T(8,128)}) custom-call(f32[128,128]{1,0:T(8,128)S(1)} %get-tuple-element.9.refs_0_, f32[128,512]{1,0:T(8,128)S(1)} %get-tuple-element.10.refs_1_, bf16[256,512]{1,0:T(8,128)(2,1)S(1)} %get-tuple-element.11.refs_2_, bf16[128,512]{1,0:T(8,128)(2,1)S(1)} %get-tuple-element.12.refs_3_, ...), custom_call_target="tpu_custom_call" | custom-call | tf_op jit(solution)/shard_map/pallas_call | solution.py:403
